TPU v7x, 32 devices: a whole 2x2x4 slice. The times are simulated.
32 devices in a mesh: head: 2 (over y), tok: 16 (over z, x, core).
Axes of the slice: x: 2, y: 2, z: 4, core: 2. Of those that a mesh axis runs over, the one named last changes fastest.
Arguments:
- queries: bfloat16 [2, 16, 4096, 256], P(None, 'head', 'tok'), may hold values from -6 to 6
- key_vectors: bfloat16 [2, 16, 4096, 256], P(None, 'head', 'tok'), may hold values from -6 to 6
- value_vectors: bfloat16 [2, 16, 4096, 256], P(None, 'head', 'tok'), may hold values from -6 to 6
- step_rates: bfloat16 [2, 16, 4096], P(None, 'head', 'tok'), may hold values from 0.029907227 to 0.29882812
- counts: int32 [2, 16], replicated, may hold values from 1 to 256, 2560 in all within a row
- out_gain: float32 [16, 256], P('head'), may hold values from 0.25 to 1.75
- w_gate: float32 [16, 512, 256], P('head', 'tok'), may hold values from -0.375 to 0.375
- w_up: float32 [16, 512, 256], P('head', 'tok'), may hold values from -0.375 to 0.375
- w_down: float32 [16, 256, 512], P('head', 'tok'), may hold values from -0.25 to 0.25
Outputs:
- mixed_out: bfloat16 [2, 16, 4096, 256], P(None, 'head', 'tok')
- final_gate: float32 [16, 512, 256], P('head', 'tok')
- final_up: float32 [16, 512, 256], P('head', 'tok')
- final_down: float32 [16, 256, 512], P('head', 'tok')
Inputs may be any that keep to these rules, and one draw needn't show every extreme that they name: `counts`: the valid tokens are the first ones of each block of 256; each row sums to 256 * 16 * 5 // 8 and some block of each group is full.
All inputs are finite; a program needn't handle non-finite values.
Results may differ from a plain program's by a relative error of at most 0.011.
Values may be sent and summed in bfloat16 or wider, within the bound.
A program may use at most 128 MiB of HBM per device.

v0:
```python
import jax
import jax.numpy as jnp
from jax import lax
from jax.sharding import PartitionSpec as P

HEADS = 16
DH = 256


epsilon = 1e-06


def renorm(previous, stepped):
    kept_norm = jnp.sqrt(jnp.mean(previous * previous, axis=-1, keepdims=True))
    return (
        stepped
        * kept_norm
        * lax.rsqrt(jnp.mean(stepped * stepped, axis=-1, keepdims=True) + epsilon)
    )


def local_terms(fast, key_rows, value_rows, rate_rows, valid_mask, grad_scale):
    gate_pre = jnp.einsum("hsd,hfd->hsf", key_rows, fast[0], preferred_element_type=jnp.float32)
    up_pre = jnp.einsum("hsd,hfd->hsf", key_rows, fast[1], preferred_element_type=jnp.float32)
    sigmoid_gate = jax.nn.sigmoid(gate_pre)
    activated = gate_pre * sigmoid_gate
    hidden = (activated * up_pre).astype(jnp.bfloat16)
    weighted = (
        value_rows.astype(jnp.float32)
        * (rate_rows.astype(jnp.float32) * grad_scale * valid_mask[None, :])[:, :, None]
    ).astype(jnp.bfloat16)
    back = jnp.einsum("hsd,hdf->hsf", weighted, fast[2], preferred_element_type=jnp.float32)
    grad_gate = (back * up_pre * sigmoid_gate * (1.0 + gate_pre * (1.0 - sigmoid_gate))).astype(
        jnp.bfloat16
    )
    grad_up = (back * activated).astype(jnp.bfloat16)
    upd_gate = jnp.einsum("hsf,hsd->hfd", grad_gate, key_rows, preferred_element_type=jnp.float32)
    upd_up = jnp.einsum("hsf,hsd->hfd", grad_up, key_rows, preferred_element_type=jnp.float32)
    upd_down = jnp.einsum("hsd,hsf->hdf", weighted, hidden, preferred_element_type=jnp.float32)
    return (upd_gate, upd_up, upd_down)


def apply_terms(fast, query_rows, valid_mask):
    gate_pre = jnp.einsum("hsd,hfd->hsf", query_rows, fast[0], preferred_element_type=jnp.float32)
    up_pre = jnp.einsum("hsd,hfd->hsf", query_rows, fast[1], preferred_element_type=jnp.float32)
    hidden = (gate_pre * jax.nn.sigmoid(gate_pre) * up_pre).astype(jnp.bfloat16)
    produced = jnp.einsum("hsf,hdf->hsd", hidden, fast[2], preferred_element_type=jnp.float32)
    return produced * valid_mask[None, :, None]


def add_terms(totals, local_sums):
    return tuple((former + latter for former, latter in zip(totals, local_sums)))


def on_device(
    queries, key_vectors, value_vectors, step_rates, counts, out_gain, w_gate, w_up, w_down
):
    tok_count = lax.axis_size("tok")
    head_count = key_vectors.shape[1]
    block = key_vectors.shape[2]
    width = key_vectors.shape[3]
    hidden_units = w_down.shape[2]
    sub_rows = min(256, block)
    grad_scale = float(tok_count * block) ** (-0.5)
    device = lax.axis_index("tok")
    gate_rows = w_gate.shape[1]
    down_rows = w_down.shape[1]
    zero_terms = (
        jnp.zeros((head_count, hidden_units, width), jnp.float32),
        jnp.zeros((head_count, hidden_units, width), jnp.float32),
        jnp.zeros((head_count, width, hidden_units), jnp.float32),
    )
    masters = (
        lax.all_gather(w_gate, "tok", axis=1, tiled=True),
        lax.all_gather(w_up, "tok", axis=1, tiled=True),
        lax.all_gather(w_down, "tok", axis=1, tiled=True),
    )
    fast = tuple((weight_set.astype(jnp.bfloat16) for weight_set in masters))
    outputs = []
    for group in range(key_vectors.shape[0]):
        valid_row = counts[group]
        own_count = valid_row[device]
        key_rows = key_vectors[group]
        value_rows = value_vectors[group]
        rate_rows = step_rates[group]
        own_subs = (own_count + sub_rows - 1) // sub_rows

        def own_step(position, totals):
            row_start = (position * sub_rows).astype(jnp.int32)
            valid_mask = (row_start + jnp.arange(sub_rows, dtype=jnp.int32) < own_count).astype(
                jnp.float32
            )
            return add_terms(
                totals, local_terms(fast, key_rows, value_rows, rate_rows, valid_mask, grad_scale)
            )

        updates = lax.fori_loop(0, own_subs, own_step, zero_terms)
        summed = lax.psum((updates[0], updates[1], updates[2]), "tok")
        masters = tuple(
            (renorm(previous, previous + update) for previous, update in zip(masters, summed))
        )
        fast = tuple((weight_set.astype(jnp.bfloat16) for weight_set in masters))
        query_rows = queries[group]
        query_subs = (own_count + sub_rows - 1) // sub_rows

        def apply_step(position, buffer):
            row_start = (position * sub_rows).astype(jnp.int32)
            valid_mask = (row_start + jnp.arange(sub_rows, dtype=jnp.int32) < own_count).astype(
                jnp.float32
            )
            produced = apply_terms(fast, query_rows, valid_mask)
            return produced

        heads_out = lax.fori_loop(
            0, query_subs, apply_step, jnp.zeros((head_count, block, width), jnp.float32)
        )
        squares = jnp.sum(heads_out * heads_out, axis=(0, 2))
        total_squares = lax.psum(squares, "head")
        mean_square = total_squares / (HEADS * DH)
        normed = (
            heads_out * out_gain[:, None, :] * lax.rsqrt(mean_square + epsilon)[None, :, None]
        ).astype(jnp.bfloat16)
        outputs.append(normed)
    final_gate = lax.dynamic_slice_in_dim(masters[0], device * gate_rows, gate_rows, 1)
    final_up = lax.dynamic_slice_in_dim(masters[1], device * gate_rows, gate_rows, 1)
    final_down = lax.dynamic_slice_in_dim(masters[2], device * down_rows, down_rows, 1)
    return (jnp.stack(outputs), final_gate, final_up, final_down)


def solution(mesh):
    in_specs = (
        P(None, "head", "tok", None),
        P(None, "head", "tok", None),
        P(None, "head", "tok", None),
        P(None, "head", "tok"),
        P(),
        P("head", None),
        P("head", "tok", None),
        P("head", "tok", None),
        P("head", "tok", None),
    )
    out_specs = (
        P(None, "head", "tok", None),
        P("head", "tok", None),
        P("head", "tok", None),
        P("head", "tok", None),
    )
    return jax.shard_map(
        on_device, mesh=mesh, in_specs=in_specs, out_specs=out_specs, check_vma=False
    )
```

profile of v0, /device:TPU:0, one launch (start us, length us, event | category | flops | bytes accessed | tf_op | source)
XLA Modules:
  0.0 771.5 jit_solution(7972449426019541128)
XLA Ops:
  11.5 2.7 fusion.53
  17.3 46.2 %all-gather.6.cloned.1.call-done = f32[8,256,512]{2,1,0:T(8,128)} async-done(((f32[8,16,512]{2,1,0:T(8,128)}), f32[8,256,512]{2,1,0:T(8,128)}) %all-gather.6.cloned.1.call-update) | async-done | bytes 4194320 | tf_op jit(solution)/shard_map/all_gather | solution.py:76
  63.5 3.8 convert_element_type.115
  67.3 47.5 %all-gather.8.cloned.1.call-done = f32[8,512,256]{2,1,0:T(8,128)} async-done(((f32[8,32,256]{2,1,0:T(8,128)}), f32[8,512,256]{2,1,0:T(8,128)}) %all-gather.8.cloned.1.call-update) | async-done | bytes 4194320 | tf_op jit(solution)/shard_map/all_gather | solution.py:75
  117.2 48.9 %all-gather.4.cloned.1.call-done = f32[8,512,256]{2,1,0:T(8,128)} async-done(((f32[8,32,256]{2,1,0:T(8,128)}), f32[8,512,256]{2,1,0:T(8,128)}) %all-gather.4.cloned.1.call-update) | async-done | bytes 4194320 | tf_op jit(solution)/shard_map/all_gather | solution.py:74
  166.1 3.7 convert_element_type.117
  174.5 2.6 broadcast_in_dim.2.clone
  177.1 22.3 %while.52 = (s32[]{:T(128)}, f32[8,512,256]{2,1,0:T(8,128)}, f32[8,512,256]{2,1,0:T(8,128)}, f32[8,256,512]{2,1,0:T(8,128)}, s32[]{:T(128)}, /*index=5*/bf16[8,2...) while((s32[]{:T(128)}, f32[8,512,256]{2,1,0:T(8,128)}, ...), condition=%wide.region_1.2_spmd, body=%wide.region_0.1_spmd.sunk | while | flops 3250590464 | bytes 92305616 | solution.py:97
  177.9 2.7 fusion.104
  182.1 5.3 convolution_add_fusion.12
  187.4 5.9 convolution_add_fusion.13
  193.3 6.0 convolution_add_fusion.14
  201.9 230.3 %all-reduce.8.cloned.1.call-done = (f32[8,256,512]{2,1,0:T(8,128)}, f32[8,512,256]{2,1,0:T(8,128)}, f32[8,512,256]{2,1,0:T(8,128)}) async-done(((f32[8,256,512]{2,1,0:T(8,128)}, f32[8,512,256]{2,1,0:T(8,128)}, f32[8,512,256]{2,1,0:T(8,128)}), (f32[8,256,512]{2,1,0:T(8,128)}, f32[8,512,256]{2,1,0:T(8,128)}, f32[8,512,256]{2,1,0:T(8,128)})) %all-reduce.8.cloned.1.call-update) | async-done | bytes 12582928 | tf_op jit(solution)/shard_map/psum | solution.py:98
  432.2 4.8 multiply_reduce_fusion.8
  444.4 2.5 fusion.25
  454.8 2.6 broadcast_in_dim.2
  457.4 23.0 %while.54 = (s32[]{:T(128)}, f32[8,512,256]{2,1,0:T(8,128)}, f32[8,512,256]{2,1,0:T(8,128)}, f32[8,256,512]{2,1,0:T(8,128)}, s32[]{:T(128)}, /*index=5*/bf16[8,2...) while((s32[]{:T(128)}, f32[8,512,256]{2,1,0:T(8,128)}, ...), condition=%wide.region_16.17_spmd, body=%wide.region_15.16_spmd.sunk | while | flops 3250590464 | bytes 92305616 | solution.py:97
  458.1 2.7 fusion.114
  463.1 5.3 convolution_add_fusion.15
  468.4 5.9 convolution_add_fusion.16
  474.4 6.0 convolution_add_fusion.17
  480.4 4.0 fusion.43
  484.4 6.4 fusion.33
  496.3 218.2 %all-reduce.6.cloned.1.call-done = (f32[8,256,512]{2,1,0:T(8,128)}, f32[8,512,256]{2,1,0:T(8,128)}, f32[8,512,256]{2,1,0:T(8,128)}) async-done(((f32[8,256,512]{2,1,0:T(8,128)}, f32[8,512,256]{2,1,0:T(8,128)}, f32[8,512,256]{2,1,0:T(8,128)}), (f32[8,256,512]{2,1,0:T(8,128)}, f32[8,512,256]{2,1,0:T(8,128)}, f32[8,512,256]{2,1,0:T(8,128)})) %all-reduce.6.cloned.1.call-update) | async-done | bytes 12582928 | tf_op jit(solution)/shard_map/psum | solution.py:98
  714.5 4.8 multiply_reduce_fusion.3
  722.9 2.5 multiply_multiply_fusion.2
  725.5 2.9 fusion.31
  734.0 2.5 multiply_multiply_fusion.1
  738.6 3.2 multiply_multiply_fusion
  741.7 6.8 fusion.28
  754.1 4.9 all-reduce.2
  760.8 2.7 fusion.36
  (137 shorter events, 65.8 us)
Async XLA Ops:
  7.2 8.4 %copy-start.36 = (bf16[2,8,256]{2,1,0:T(8,128)(2,1)S(1)}, bf16[2,8,256]{2,1,0:T(8,128)(2,1)}, u32[]{:S(2)}) copy-start(bf16[2,8,256]{2,1,0:T(8,128)(2,1)} %param.20) | copy-start | bytes 24580
  7.2 8.9 %copy-start.21 = (bf16[2,8,256,256]{3,2,1,0:T(8,128)(2,1)S(1)}, bf16[2,8,256,256]{3,2,1,0:T(8,128)(2,1)}, u32[]{:S(2)}) copy-start(bf16[2,8,256,256]{3,2,1,0:T(8,128)(2,1)} %param.18) | copy-start | bytes 6291460
  7.2 56.3 %all-gather.6.cloned.1.call-start = ((), (), s32[]{:S(2)}) async-start(), calls=%async_computation.1 | async-start | bytes 4456448 | tf_op jit(solution)/shard_map/all_gather | solution.py:76
  7.9 106.9 %all-gather.8.cloned.1.call-start = ((), (), s32[]{:S(2)}) async-start(), calls=%async_computation.2 | async-start | bytes 4456448 | tf_op jit(solution)/shard_map/all_gather | solution.py:75
  8.7 157.4 %all-gather.4.cloned.1.call-start = ((), (), s32[]{:S(2)}) async-start(), calls=%async_computation | async-start | bytes 4456448 | tf_op jit(solution)/shard_map/all_gather | solution.py:74
  9.4 422.8 %all-reduce.8.cloned.1.call-start = ((), (), s32[]{:S(2)}) async-start(), calls=%async_computation.4 | async-start | bytes 25165824 | tf_op jit(solution)/shard_map/psum | solution.py:98
  187.4 5.9 copy-start.10
  199.4 515.1 %all-reduce.6.cloned.1.call-start = ((), (), s32[]{:S(2)}) async-start(), calls=%async_computation.3 | async-start | bytes 25165824 | tf_op jit(solution)/shard_map/psum | solution.py:98
  432.2 4.9 copy-start.11
  432.2 6.1 copy-start.17
  437.0 7.4 copy-start.3
  437.1 7.4 copy-start.22
  437.1 7.3 copy-start.24
  438.3 5.2 copy-start.18
  439.6 7.4 copy-start.5
  439.6 7.4 copy-start.26
  439.6 7.4 copy-start.28
  444.4 4.1 copy-start.7
  444.4 4.1 copy-start.31
  452.5 4.9 copy-start
  452.5 4.9 copy-start.30
  468.4 5.9 copy-start.9
  492.2 222.3 %copy-start.23 = (f32[8,512]{1,0:T(8,128)S(1)}, f32[8,512]{1,0:T(8,128)}, u32[]{:S(2)}) copy-start(f32[8,512]{1,0:T(8,128)} %copy-done.22) | copy-start | bytes 49156
  492.2 222.3 %copy-start.25 = (f32[8,512]{1,0:T(8,128)S(1)}, f32[8,512]{1,0:T(8,128)}, u32[]{:S(2)}) copy-start(f32[8,512]{1,0:T(8,128)} %copy-done.24) | copy-start | bytes 49156
  714.5 4.9 copy-start.6
  714.5 5.9 copy-start.14
  714.5 5.9 copy-start.27
  714.5 5.9 copy-start.29
  725.4 5.0 copy-start.12
  725.4 5.0 copy-start.32
  725.4 5.0 copy-start.34
  750.1 10.7 %copy-start.35 = (f32[8,256]{1,0:T(8,128)S(1)}, f32[8,256]{1,0:T(8,128)}, u32[]{:S(2)}) copy-start(f32[8,256]{1,0:T(8,128)} %param.22) | copy-start | bytes 24580
  (10 other events, 27.2 us)
Sparse Core Ops, SparseCore 0:
  10.2 53.2 all-gather.5
  65.7 49.0 all-gather.7
  117.0 49.0 all-gather.3
  199.5 232.6 all-reduce.7
  480.5 233.9 all-reduce.5
where the time goes:
time: 772 us; the launch traced here: 771 us
  waiting for transfers between devices  593 us (77%)
  matrix products  62.9 us (8%)
  other arithmetic  53 us (7%)
  local copies, waits for them, and re-layouts  41.3 us (5%)
  between operations  15.6 us (2%)
    psum x2, waiting for transfers between devices, on_device(): summed = lax.psum((updates[0], updates[1], updates[2]), 'tok')  449 us
    all_gather x1, waiting for transfers between devices, on_device(): lax.all_gather(w_gate, 'tok', axis=1, tiled=True)  48.9 us
    all_gather x1, waiting for transfers between devices, on_device(): lax.all_gather(w_up, 'tok', axis=1, tiled=True)  47.5 us
    all_gather x1, waiting for transfers between devices, on_device(): lax.all_gather(w_down, 'tok', axis=1, tiled=True)  46.2 us
    convert_element_type x6, other arithmetic, on_device(): fast = tuple((weight_set.astype(jnp.bfloat16) for weight_set in masters))  15.6 us
  transfers between devices with their start and end apart: 5, of which 5 were waited for; matrix products, arithmetic and copies ran while one was open for 4% of the time, Pallas kernels for 0%

commit v1 on v0

v1 whole, which is shorter than its diff:
```python
import functools

import jax
import jax.numpy as jnp
from jax import lax
from jax.experimental import pallas as pl
from jax.experimental.pallas import tpu as pltpu
from jax.sharding import PartitionSpec as P

epsilon = 1e-06
MESH = pl.DeviceIdType.MESH
NT = (((1,), (1,)), ((), ()))


def dot_nt(left, right):
    return lax.dot_general(left, right, NT, preferred_element_type=jnp.float32)


def dot_nn(left, right):
    return jnp.dot(left, right, preferred_element_type=jnp.float32)


def sigmoid(x):
    return 0.5 * jnp.tanh(0.5 * x) + 0.5


def renorm(previous, stepped):
    kept = jnp.sqrt(jnp.mean(previous * previous, axis=-1, keepdims=True))
    return (
        stepped
        * kept
        * lax.rsqrt(jnp.mean(stepped * stepped, axis=-1, keepdims=True) + epsilon)
    )


def kernel(
    dims,
    k_ref, e_ref, q_ref, mask_ref, gain_ref, wg_ref, wu_ref, wd_ref,
    out_ref, fg_ref, fu_ref, fd_ref,
    kbuf, ebuf, qbuf, o_send, o_recv,
    gu_m, d_m, gu_b, d_b, dt_b,
    dgu, ddt, dd,
    rs_send, rs_recv, rsd_send, rsd_recv,
    ms_send, ms_recv,
    tok_s, tok_r, w_s, w_r, o_s, o_r, f_s, f_r,
    rs_s, rs_r, ag_s, ag_r, ms_s, ms_r,
):
    tok_n, head_n, parts, reps, per = dims
    groups = k_ref.shape[0]
    heads = k_ref.shape[1]
    width = k_ref.shape[3]
    hidden = wd_ref.shape[2]
    gate_rows, down_rows = wg_ref.shape[1], wd_ref.shape[1]
    gate_part, down_part = parts * gate_rows, parts * down_rows
    tok = lax.axis_index("tok")
    hid = lax.axis_index("head")
    mine = lax.rem(tok, parts)
    rep = tok // parts

    part_peers = [lax.rem(mine + s, parts) for s in range(1, parts)]
    rep_peers = [lax.rem(rep + s, reps) for s in range(1, reps)]
    head_peers = [lax.rem(hid + s, head_n) for s in range(1, head_n)]

    def part_dev(index):
        return (hid, rep * parts + index)

    def rep_dev(index):
        return (hid, index * parts + mine)

    barrier = pltpu.get_barrier_semaphore()
    everyone = (
        [part_dev(j) for j in part_peers]
        + [rep_dev(j) for j in rep_peers]
        + [(j, tok) for j in head_peers]
    )
    for device in everyone:
        pl.semaphore_signal(barrier, inc=1, device_id=device, device_id_type=MESH)
    pl.semaphore_wait(barrier, len(everyone))

    pending = []

    def remote(src, dst, send, recv, device):
        return pltpu.make_async_remote_copy(
            src_ref=src, dst_ref=dst, send_sem=send, recv_sem=recv,
            device_id=device, device_id_type=MESH,
        )

    def push(src, dst, send, recv, device):
        copy = remote(src, dst, send, recv, device)
        copy.start()
        pending.append(copy)

    def rows_of(index, size):
        return pl.ds(pl.multiple_of(index * size, size), size)

    def heads_of(index):
        return pl.ds(index * per, per)

    tokens = ((k_ref, kbuf), (e_ref, ebuf), (q_ref, qbuf))

    def send_tokens(group, kinds):
        for s, j in enumerate(part_peers):
            for kind in kinds:
                src, dst = tokens[kind]
                push(
                    src.at[group, heads_of(j)], dst.at[group, mine],
                    tok_s.at[group, kind, s], tok_r.at[group, kind, s], part_dev(j),
                )

    def wait_tokens(group, kinds, source, s):
        for kind in kinds:
            dst = tokens[kind][1].at[group, source]
            remote(
                dst, dst, tok_s.at[group, kind, s], tok_r.at[group, kind, s], part_dev(source)
            ).wait_recv()

    weights = (
        (wg_ref, gu_m.at[0], gate_rows), (wu_ref, gu_m.at[1], gate_rows), (wd_ref, d_m, down_rows)
    )
    for s, j in enumerate(part_peers):
        for kind, (src, dst, rows) in enumerate(weights):
            push(
                src.at[heads_of(j)], dst.at[:, rows_of(mine, rows)],
                w_s.at[kind, s], w_r.at[kind, s], part_dev(j),
            )
    send_tokens(0, (0, 1))
    send_tokens(0, (2,))
    for src, dst, rows in weights:
        dst[:, rows_of(mine, rows)] = src[heads_of(mine)]
    for group in range(groups):
        for src, dst in tokens:
            dst[group, mine] = src[group, heads_of(mine)]

    def share(stage):
        gate_own, down_own = rows_of(rep, gate_part), rows_of(rep, down_part)
        gu_b[stage, :, :, gate_own] = gu_m[...].astype(jnp.bfloat16)
        d_b[stage, :, down_own] = d_m[...].astype(jnp.bfloat16)
        for s, j in enumerate(rep_peers):
            gu = gu_b.at[stage, :, :, gate_own]
            push(gu, gu, ag_s.at[stage, 0, s], ag_r.at[stage, 0, s], rep_dev(j))
            down = d_b.at[stage, :, down_own]
            push(down, down, ag_s.at[stage, 1, s], ag_r.at[stage, 1, s], rep_dev(j))

    def wait_share(stage):
        for s in range(reps - 1):
            j = lax.rem(rep + reps - 1 - s, reps)
            gu = gu_b.at[stage, :, :, rows_of(j, gate_part)]
            remote(gu, gu, ag_s.at[stage, 0, s], ag_r.at[stage, 0, s], rep_dev(j)).wait_recv()
            down = d_b.at[stage, :, rows_of(j, down_part)]
            remote(down, down, ag_s.at[stage, 1, s], ag_r.at[stage, 1, s], rep_dev(j)).wait_recv()

    def update(group):
        dgu[...] = jnp.zeros_like(dgu)
        ddt[...] = jnp.zeros_like(ddt)
        for h in range(per):
            dt_b[h] = d_b[group, h].astype(jnp.float32).T.astype(jnp.bfloat16)

        def one(source):
            for h in range(per):
                key = kbuf[group, source, h]
                err = ebuf[group, source, h]
                a = dot_nt(gu_b[group, 0, h], key)
                b = dot_nt(gu_b[group, 1, h], key)
                r = dot_nt(dt_b[h], err)
                sg = sigmoid(a)
                act = a * sg
                ddt[h] += dot_nn((act * b).astype(jnp.bfloat16), err)
                da = (r * b * sg * (1.0 + a * (1.0 - sg))).astype(jnp.bfloat16)
                dgu[0, h] += dot_nn(da, key)
                dgu[1, h] += dot_nn((r * act).astype(jnp.bfloat16), key)

        def step(s, carry):
            source = lax.rem(mine + parts - s, parts)

            @pl.when(s > 0)
            def _():
                wait_tokens(group, (0, 1), source, s - 1)

            one(source)
            return carry

        lax.fori_loop(0, parts, step, 0)
        for h in range(per):
            dd[h] = ddt[h].T

    def scatter(group):
        for s, j in enumerate(rep_peers):
            rs_send[group, s] = dgu[:, :, rows_of(j, gate_part)].astype(jnp.bfloat16)
            push(
                rs_send.at[group, s], rs_recv.at[group, s],
                rs_s.at[group, 0, s], rs_r.at[group, 0, s], rep_dev(j),
            )
            rsd_send[group, s] = dd[:, rows_of(j, down_part)].astype(jnp.bfloat16)
            push(
                rsd_send.at[group, s], rsd_recv.at[group, s],
                rs_s.at[group, 1, s], rs_r.at[group, 1, s], rep_dev(j),
            )

    def settle(group):
        gate = gu_m[...] + dgu[:, :, rows_of(rep, gate_part)]
        down = d_m[...] + dd[:, rows_of(rep, down_part)]
        for s in range(reps - 1):
            j = lax.rem(rep + reps - 1 - s, reps)
            got = rs_recv.at[group, s]
            remote(got, got, rs_s.at[group, 0, s], rs_r.at[group, 0, s], rep_dev(j)).wait_recv()
            gate = gate + got[...].astype(jnp.float32)
            got = rsd_recv.at[group, s]
            remote(got, got, rs_s.at[group, 1, s], rs_r.at[group, 1, s], rep_dev(j)).wait_recv()
            down = down + got[...].astype(jnp.float32)
        gu_m[...] = renorm(gu_m[...], gate)
        d_m[...] = renorm(d_m[...], down)

    def apply(group):
        stage = group + 1

        def one(source, into):
            for h in range(per):
                query = qbuf[group, source, h]
                a = dot_nt(query, gu_b[stage, 0, h])
                b = dot_nt(query, gu_b[stage, 1, h])
                hid_act = (a * sigmoid(a) * b).astype(jnp.bfloat16)
                into[h] = dot_nt(hid_act, d_b[stage, h]).astype(jnp.bfloat16)

        def out_copy(s):
            source = lax.rem(mine + parts - 1 - s, parts)
            return remote(
                o_send.at[group, s], o_recv.at[group, mine],
                o_s.at[group, s], o_r.at[group, s], part_dev(source),
            )

        def step(s, carry):
            source = lax.rem(mine + parts - 1 - s, parts)
            wait_tokens(group, (2,), source, s)
            one(source, o_send.at[group, s])
            out_copy(s).start()
            return carry

        lax.fori_loop(0, parts - 1, step, 0)
        one(mine, o_recv.at[group, mine])
        for s in range(parts - 1):
            pending.append(out_copy(s))

    def finish(group):
        for s, j in enumerate(part_peers):
            got = o_recv.at[group, j]
            remote(got, got, o_s.at[group, s], o_r.at[group, s], part_dev(j)).wait_recv()
        half = width // 2
        total = jnp.zeros((k_ref.shape[2], half), jnp.float32)
        for head in range(heads):
            o = o_recv[group, head // per, head % per].astype(jnp.float32)
            total = total + (o[:, :half] * o[:, :half] + o[:, half:] * o[:, half:])
        ms_send[group] = total
        for s, j in enumerate(head_peers):
            push(
                ms_send.at[group], ms_recv.at[group, s],
                ms_s.at[group, s], ms_r.at[group, s], (j, tok),
            )
        for s in range(head_n - 1):
            j = lax.rem(hid + head_n - 1 - s, head_n)
            got = ms_recv.at[group, s]
            remote(got, got, ms_s.at[group, s], ms_r.at[group, s], (j, tok)).wait_recv()
            total = total + got[...]
        mean = jnp.sum(total, axis=1, keepdims=True) / (head_n * heads * width)
        scale = lax.rsqrt(mean + epsilon) * mask_ref[group]
        for head in range(heads):
            o = o_recv[group, head // per, head % per].astype(jnp.float32)
            out_ref[group, head] = (o * gain_ref[pl.ds(head, 1), :] * scale).astype(jnp.bfloat16)

    for s in range(parts - 1):
        j = lax.rem(mine + parts - 1 - s, parts)
        for kind, (_, dst, rows) in enumerate(weights):
            got = dst.at[:, rows_of(j, rows)]
            remote(got, got, w_s.at[kind, s], w_r.at[kind, s], part_dev(j)).wait_recv()
    share(0)
    wait_share(0)
    for group in range(groups):
        update(group)
        scatter(group)
        if group + 1 < groups:
            send_tokens(group + 1, (0, 1, 2))
        if group > 0:
            apply(group - 1)
        settle(group)
        share(group + 1)
        if group > 0:
            finish(group - 1)
        if group + 1 == groups:
            finals = ((gu_m.at[0], fg_ref, gate_rows), (gu_m.at[1], fu_ref, gate_rows),
                      (d_m, fd_ref, down_rows))
            for s, j in enumerate(part_peers):
                for kind, (src, dst, rows) in enumerate(finals):
                    push(
                        src.at[:, rows_of(j, rows)], dst.at[heads_of(mine)],
                        f_s.at[kind, s], f_r.at[kind, s], part_dev(j),
                    )
            for src, dst, rows in finals:
                dst[heads_of(mine)] = src[:, rows_of(mine, rows)]
        wait_share(group + 1)
    apply(groups - 1)
    finish(groups - 1)
    for s in range(parts - 1):
        j = lax.rem(mine + parts - 1 - s, parts)
        for kind, (_, dst, rows) in enumerate(finals):
            got = dst.at[heads_of(j)]
            remote(got, got, f_s.at[kind, s], f_r.at[kind, s], part_dev(j)).wait_recv()
    for copy in pending:
        copy.wait_send()


def on_device(
    queries, key_vectors, value_vectors, step_rates, counts, out_gain, w_gate, w_up, w_down
):
    tok_n, head_n = lax.axis_size("tok"), lax.axis_size("head")
    groups, heads, block, width = key_vectors.shape
    hidden = w_down.shape[2]
    parts = min(heads, tok_n)
    per, reps = heads // parts, tok_n // parts
    gate_rows, down_rows = w_gate.shape[1], w_down.shape[1]
    gate_part, down_part = parts * gate_rows, parts * down_rows
    grad_scale = float(tok_n * block) ** (-0.5)
    own = lax.dynamic_slice_in_dim(counts, lax.axis_index("tok"), 1, 1)
    mask = (jnp.arange(block, dtype=jnp.int32)[None, :] < own).astype(jnp.float32)
    rate = step_rates.astype(jnp.float32) * grad_scale * mask[:, None, :]
    errors = (value_vectors.astype(jnp.float32) * rate[..., None]).astype(jnp.bfloat16)

    bf16, f32 = jnp.bfloat16, jnp.float32
    vmem, dma = pltpu.VMEM, pltpu.SemaphoreType.DMA
    pn, rn, hn = max(parts - 1, 1), max(reps - 1, 1), max(head_n - 1, 1)
    scratch = [
        vmem((groups, parts, per, block, width), bf16),
        vmem((groups, parts, per, block, width), bf16),
        vmem((groups, parts, per, block, width), bf16),
        vmem((groups, pn, per, block, width), bf16),
        vmem((groups, parts, per, block, width), bf16),
        vmem((2, per, gate_part, width), f32),
        vmem((per, down_part, hidden), f32),
        vmem((groups + 1, 2, per, hidden, width), bf16),
        vmem((groups + 1, per, width, hidden), bf16),
        vmem((per, hidden, width), bf16),
        vmem((2, per, hidden, width), f32),
        vmem((per, hidden, width), f32),
        vmem((per, width, hidden), f32),
        vmem((groups, rn, 2, per, gate_part, width), bf16),
        vmem((groups, rn, 2, per, gate_part, width), bf16),
        vmem((groups, rn, per, down_part, hidden), bf16),
        vmem((groups, rn, per, down_part, hidden), bf16),
        vmem((groups, block, width // 2), f32),
        vmem((groups, hn, block, width // 2), f32),
        dma((groups, 3, pn)), dma((groups, 3, pn)),
        dma((3, pn)), dma((3, pn)),
        dma((groups, pn)), dma((groups, pn)),
        dma((3, pn)), dma((3, pn)),
        dma((groups, 2, rn)), dma((groups, 2, rn)),
        dma((groups + 1, 2, rn)), dma((groups + 1, 2, rn)),
        dma((groups, hn)), dma((groups, hn)),
    ]
    whole = pl.BlockSpec(memory_space=pltpu.VMEM)
    flops = groups * heads * 9 * 2 * block * width * hidden
    return pl.pallas_call(
        functools.partial(kernel, (tok_n, head_n, parts, reps, per)),
        out_shape=(
            jax.ShapeDtypeStruct(queries.shape, bf16),
            jax.ShapeDtypeStruct(w_gate.shape, f32),
            jax.ShapeDtypeStruct(w_up.shape, f32),
            jax.ShapeDtypeStruct(w_down.shape, f32),
        ),
        in_specs=[whole] * 8,
        out_specs=(whole,) * 4,
        scratch_shapes=scratch,
        cost_estimate=pl.CostEstimate(
            flops=flops, bytes_accessed=8 * queries.size, transcendentals=0
        ),
        compiler_params=pltpu.CompilerParams(
            collective_id=0, has_side_effects=True, vmem_limit_bytes=56 * 1024 * 1024
        ),
    )(key_vectors, errors, queries, mask[..., None], out_gain, w_gate, w_up, w_down)


def solution(mesh):
    tokens = P(None, "head", "tok", None)
    weight = P("head", "tok", None)
    in_specs = (
        tokens, tokens, tokens, P(None, "head", "tok"), P(), P("head", None),
        weight, weight, weight,
    )
    return jax.shard_map(
        on_device, mesh=mesh, in_specs=in_specs,
        out_specs=(tokens, weight, weight, weight), check_vma=False,
    )
```

time: 772 us -> 188 us (0.24)
  waiting for transfers between devices: 593 us -> 0 us
  Pallas kernels: 0 us -> 176 us
  matrix products: 62.9 us -> 0 us
  other arithmetic: 53 us -> 4.46 us
  local copies, waits for them, and re-layouts: 41.3 us -> 6.14 us
  between operations: 15.6 us -> 0.68 us
    psum x2 -> x0, waiting for transfers between devices: 449 us -> none  [on_device(): summed = lax.psum((updates[0], updates[1], updates[2]), 'tok')]
    pallas_call x0 -> x1, Pallas kernels: none -> 176 us  [on_device(): pl.pallas_call(functools.partial(kernel, (tok_n, head_n, parts, reps, per...]
    all_gather x3 -> x0, waiting for transfers between devices: 143 us -> none  [the longest x1 48.9 us: on_device(): lax.all_gather(w_gate, 'tok', axis=1, tiled=True)]
    dot_general x16 -> x0, matrix products: 62.9 us -> none  [the longest x2 13.2 us: apply_terms(): jnp.einsum('hsf,hdf->hsd', hidden, fast[2], preferred_element_type=jnp.fl...]
    reduce_sum x8 -> x0, other arithmetic: 19.1 us -> none  [the longest x3 8.65 us: renorm(): kept_norm = jnp.sqrt(jnp.mean(previous * previous, axis=-1, keepdims=True))]
    convert_element_type x8 -> x2, other arithmetic: 16.9 us -> 3.68 us  [the longest x1 2.89 us: on_device(): (value_vectors.astype(jnp.float32) * rate[..., None]).astype(jnp.bfloat16)]
    another operation x6 -> x0, local copies, waits for them, and re-layouts: 12.3 us -> none
    mul x9 -> x2, other arithmetic: 12.7 us -> 0.78 us  [on_device(): rate = step_rates.astype(jnp.float32) * grad_scale * mask[:, None, :]]
  transfers between devices with their start and end apart: 5 -> 0, of which waited for: 5 -> 0; matrix products, arithmetic and copies ran while one was open for 4% -> 0% of each run, Pallas kernels for 0% -> 0%
where the time goes in v1:
time: 188 us; the launch traced here: 187 us
  Pallas kernels  176 us (94%)
  local copies, waits for them, and re-layouts  6.14 us (3%)
  other arithmetic  4.46 us (2%)
    pallas_call x1, Pallas kernels, on_device(): pl.pallas_call(functools.partial(kernel, (tok_n, head_n, parts, reps, per...  176 us
    unnamed x12, local copies, waits for them, and re-layouts  5.96 us

profile of v1, /device:TPU:0, one launch (start us, length us, event | category | flops | bytes accessed | tf_op | source)
XLA Modules:
  0.0 187.4 jit_solution(936981957365324327)
XLA Ops:
  0.6 0.0 copy-start
  0.6 0.7 copy-done
  1.3 0.2 dynamic-slice_reduce_fusion
  1.5 0.1 compare_select_fusion
  1.6 0.7 convert_multiply_fusion
  2.3 0.8 fusion.mask_ref
  3.1 2.9 %multiply_convert_fusion.e_ref = bf16[2,8,256,256]{3,2,1,0:T(8,128)(2,1)} fusion(bf16[2,8,256,256]{3,2,1,0:T(8,128)(2,1)} %param.11, f32[2,8,256]{2,1,0:T(8,128)S(1)} %convert_multiply_fusion), kind=kLoop, calls=%fused_computation | loop fusion | flops 3145728 | bytes 4210688 | tf_op jit(solution)/shard_map/convert_element_type | solution.py:324
  6.0 176.1 %shard_map.120 = (bf16[2,8,256,256]{3,2,1,0:T(8,128)(2,1)}, f32[8,32,256]{2,1,0:T(8,128)}, f32[8,32,256]{2,1,0:T(8,128)}, f32[8,16,512]{2,1,0:T(8,128)}) custom-call(bf16[2,8,256,256]{3,2,1,0:T(8,128)(2,1)} %k_ref.1, bf16[2,8,256,256]{3,2,1,0:T(8,128)(2,1)} %multiply_convert_fusion.e_ref, bf16[2,8,256,256]{3,2,1,0:T(8,128)(2,1)} %q_ref.1, ...), custom_call_target="tpu_custom_call" | custom-call | flops 9663676416 | bytes 8388608 | tf_op jit(solution)/shard_map/pallas_call | solution.py:359
  182.1 0.0 copy-start.3
  182.1 0.0 copy-start.2
  182.1 0.0 copy-start.1
  182.1 3.2 %copy.17 = bf16[2,8,256,256]{3,2,1,0:T(8,128)(2,1)} copy(bf16[2,8,256,256]{3,2,1,0:T(8,128)(2,1)} %get-tuple-element.8) | data formatting | bytes 4194304
  185.3 0.0 copy-done.3
  185.3 0.7 copy.18
  186.0 0.0 copy-done.2
  186.0 0.7 copy.19
  186.7 0.0 copy-done.1
  186.7 0.7 copy.20
Async XLA Ops:
  0.6 0.7 copy-start
  182.1 3.2 %copy-start.3 = (f32[8,32,256]{2,1,0:T(8,128)S(1)}, f32[8,32,256]{2,1,0:T(8,128)}, u32[]{:S(2)}) copy-start(f32[8,32,256]{2,1,0:T(8,128)} %get-tuple-element.9) | copy-start | bytes 786436
  182.1 3.9 %copy-start.2 = (f32[8,32,256]{2,1,0:T(8,128)S(1)}, f32[8,32,256]{2,1,0:T(8,128)}, u32[]{:S(2)}) copy-start(f32[8,32,256]{2,1,0:T(8,128)} %get-tuple-element.10) | copy-start | bytes 786436
  182.1 4.6 %copy-start.1 = (f32[8,16,512]{2,1,0:T(8,128)S(1)}, f32[8,16,512]{2,1,0:T(8,128)}, u32[]{:S(2)}) copy-start(f32[8,16,512]{2,1,0:T(8,128)} %get-tuple-element.11) | copy-start | bytes 786436

commit v2 on v1

--- a/solution.py
+++ b/solution.py
@@ -33,11 +33,22 @@
     )
 
 
+def flip(index, step, count):
+    result = index
+    bit = 1
+    while bit < count:
+        on = lax.rem(lax.div(index, bit), 2)
+        chosen = (step // bit) % 2 if isinstance(step, int) else lax.rem(lax.div(step, bit), 2)
+        result = result + bit * chosen * (1 - 2 * on)
+        bit *= 2
+    return result
+
+
 def kernel(
     dims,
-    k_ref, e_ref, q_ref, mask_ref, gain_ref, wg_ref, wu_ref, wd_ref,
-    out_ref, fg_ref, fu_ref, fd_ref,
-    kbuf, ebuf, qbuf, o_send, o_recv,
+    k_ref, e_ref, q_ref, mask_ref, wg_ref, wu_ref, wd_ref,
+    out_ref, scale_ref, fg_ref, fu_ref, fd_ref,
+    kbuf, ebuf, qbuf, o_send, wg_c, wu_c, wd_c, fin_g, fin_u, fin_d,
     gu_m, d_m, gu_b, d_b, dt_b,
     dgu, ddt, dd,
     rs_send, rs_recv, rsd_send, rsd_recv,
@@ -57,9 +68,9 @@
     mine = lax.rem(tok, parts)
     rep = tok // parts
 
-    part_peers = [lax.rem(mine + s, parts) for s in range(1, parts)]
-    rep_peers = [lax.rem(rep + s, reps) for s in range(1, reps)]
-    head_peers = [lax.rem(hid + s, head_n) for s in range(1, head_n)]
+    part_peers = [flip(mine, s, parts) for s in range(1, parts)]
+    rep_peers = [flip(rep, s, reps) for s in range(1, reps)]
+    head_peers = [flip(hid, s, head_n) for s in range(1, head_n)]
 
     def part_dev(index):
         return (hid, rep * parts + index)
@@ -75,6 +86,9 @@
     )
     for device in everyone:
         pl.semaphore_signal(barrier, inc=1, device_id=device, device_id_type=MESH)
+    wg_c[...] = wg_ref[...].astype(wg_c.dtype)
+    wu_c[...] = wu_ref[...].astype(wu_c.dtype)
+    wd_c[...] = wd_ref[...].astype(wd_c.dtype)
     pl.semaphore_wait(barrier, len(everyone))
 
     pending = []
@@ -114,27 +128,35 @@
                 dst, dst, tok_s.at[group, kind, s], tok_r.at[group, kind, s], part_dev(source)
             ).wait_recv()
 
-    weights = (
-        (wg_ref, gu_m.at[0], gate_rows), (wu_ref, gu_m.at[1], gate_rows), (wd_ref, d_m, down_rows)
-    )
+    narrow_gate = wg_c.dtype == jnp.bfloat16
+    narrow_down = wd_c.dtype == jnp.bfloat16
+
+    def owned(stage, index):
+        row = rep * parts + index
+        if narrow_gate:
+            gate = [gu_b.at[stage, i, :, rows_of(row, gate_rows)] for i in range(2)]
+        else:
+            gate = [gu_m.at[i, :, rows_of(index, gate_rows)] for i in range(2)]
+        if narrow_down:
+            return gate + [d_b.at[stage, :, rows_of(row, down_rows)]]
+        return gate + [d_m.at[:, rows_of(index, down_rows)]]
+
     for s, j in enumerate(part_peers):
-        for kind, (src, dst, rows) in enumerate(weights):
-            push(
-                src.at[heads_of(j)], dst.at[:, rows_of(mine, rows)],
-                w_s.at[kind, s], w_r.at[kind, s], part_dev(j),
-            )
+        for kind, (src, dst) in enumerate(zip((wg_c, wu_c, wd_c), owned(0, mine))):
+            push(src.at[heads_of(j)], dst, w_s.at[kind, s], w_r.at[kind, s], part_dev(j))
     send_tokens(0, (0, 1))
-    send_tokens(0, (2,))
-    for src, dst, rows in weights:
-        dst[:, rows_of(mine, rows)] = src[heads_of(mine)]
+    for src, dst in zip((wg_c, wu_c, wd_c), owned(0, mine)):
+        dst[...] = src[heads_of(mine)]
     for group in range(groups):
         for src, dst in tokens:
             dst[group, mine] = src[group, heads_of(mine)]
 
     def share(stage):
         gate_own, down_own = rows_of(rep, gate_part), rows_of(rep, down_part)
-        gu_b[stage, :, :, gate_own] = gu_m[...].astype(jnp.bfloat16)
-        d_b[stage, :, down_own] = d_m[...].astype(jnp.bfloat16)
+        if stage > 0 or not narrow_gate:
+            gu_b[stage, :, :, gate_own] = gu_m[...].astype(jnp.bfloat16)
+        if stage > 0 or not narrow_down:
+            d_b[stage, :, down_own] = d_m[...].astype(jnp.bfloat16)
         for s, j in enumerate(rep_peers):
             gu = gu_b.at[stage, :, :, gate_own]
             push(gu, gu, ag_s.at[stage, 0, s], ag_r.at[stage, 0, s], rep_dev(j))
@@ -143,7 +165,7 @@
 
     def wait_share(stage):
         for s in range(reps - 1):
-            j = lax.rem(rep + reps - 1 - s, reps)
+            j = rep_peers[s]
             gu = gu_b.at[stage, :, :, rows_of(j, gate_part)]
             remote(gu, gu, ag_s.at[stage, 0, s], ag_r.at[stage, 0, s], rep_dev(j)).wait_recv()
             down = d_b.at[stage, :, rows_of(j, down_part)]
@@ -170,7 +192,7 @@
                 dgu[1, h] += dot_nn((r * act).astype(jnp.bfloat16), key)
 
         def step(s, carry):
-            source = lax.rem(mine + parts - s, parts)
+            source = flip(mine, s, parts)
 
             @pl.when(s > 0)
             def _():
@@ -200,7 +222,7 @@
         gate = gu_m[...] + dgu[:, :, rows_of(rep, gate_part)]
         down = d_m[...] + dd[:, rows_of(rep, down_part)]
         for s in range(reps - 1):
-            j = lax.rem(rep + reps - 1 - s, reps)
+            j = rep_peers[s]
             got = rs_recv.at[group, s]
             remote(got, got, rs_s.at[group, 0, s], rs_r.at[group, 0, s], rep_dev(j)).wait_recv()
             gate = gate + got[...].astype(jnp.float32)
@@ -222,32 +244,32 @@
                 into[h] = dot_nt(hid_act, d_b[stage, h]).astype(jnp.bfloat16)
 
         def out_copy(s):
-            source = lax.rem(mine + parts - 1 - s, parts)
             return remote(
-                o_send.at[group, s], o_recv.at[group, mine],
-                o_s.at[group, s], o_r.at[group, s], part_dev(source),
+                o_send.at[group, s], out_ref.at[group, heads_of(mine)],
+                o_s.at[group, s], o_r.at[group, s], part_dev(flip(mine, s + 1, parts)),
             )
 
-        def step(s, carry):
-            source = lax.rem(mine + parts - 1 - s, parts)
+        def step(i, carry):
+            s = parts - 2 - i
+            source = flip(mine, s + 1, parts)
             wait_tokens(group, (2,), source, s)
             one(source, o_send.at[group, s])
             out_copy(s).start()
             return carry
 
         lax.fori_loop(0, parts - 1, step, 0)
-        one(mine, o_recv.at[group, mine])
+        one(mine, out_ref.at[group, heads_of(mine)])
         for s in range(parts - 1):
             pending.append(out_copy(s))
 
     def finish(group):
         for s, j in enumerate(part_peers):
-            got = o_recv.at[group, j]
+            got = out_ref.at[group, heads_of(j)]
             remote(got, got, o_s.at[group, s], o_r.at[group, s], part_dev(j)).wait_recv()
         half = width // 2
         total = jnp.zeros((k_ref.shape[2], half), jnp.float32)
         for head in range(heads):
-            o = o_recv[group, head // per, head % per].astype(jnp.float32)
+            o = out_ref[group, head].astype(jnp.float32)
             total = total + (o[:, :half] * o[:, :half] + o[:, half:] * o[:, half:])
         ms_send[group] = total
         for s, j in enumerate(head_peers):
@@ -256,53 +278,53 @@
                 ms_s.at[group, s], ms_r.at[group, s], (j, tok),
             )
         for s in range(head_n - 1):
-            j = lax.rem(hid + head_n - 1 - s, head_n)
+            j = head_peers[s]
             got = ms_recv.at[group, s]
             remote(got, got, ms_s.at[group, s], ms_r.at[group, s], (j, tok)).wait_recv()
             total = total + got[...]
         mean = jnp.sum(total, axis=1, keepdims=True) / (head_n * heads * width)
         scale = lax.rsqrt(mean + epsilon) * mask_ref[group]
-        for head in range(heads):
-            o = o_recv[group, head // per, head % per].astype(jnp.float32)
-            out_ref[group, head] = (o * gain_ref[pl.ds(head, 1), :] * scale).astype(jnp.bfloat16)
-
-    for s in range(parts - 1):
-        j = lax.rem(mine + parts - 1 - s, parts)
-        for kind, (_, dst, rows) in enumerate(weights):
-            got = dst.at[:, rows_of(j, rows)]
+        scale_ref[group] = jnp.broadcast_to(scale, scale_ref.shape[1:])
+
+    for s, j in enumerate(part_peers):
+        for kind, got in enumerate(owned(0, j)):
             remote(got, got, w_s.at[kind, s], w_r.at[kind, s], part_dev(j)).wait_recv()
     share(0)
+    if narrow_gate:
+        gu_m[...] = gu_b[0, :, :, rows_of(rep, gate_part)].astype(jnp.float32)
+    if narrow_down:
+        d_m[...] = d_b[0, :, rows_of(rep, down_part)].astype(jnp.float32)
     wait_share(0)
+    finals = (fin_g, fin_u, fin_d)
     for group in range(groups):
         update(group)
         scatter(group)
         if group + 1 < groups:
-            send_tokens(group + 1, (0, 1, 2))
+            send_tokens(group + 1, (0, 1))
         if group > 0:
+            send_tokens(group, (2,))
             apply(group - 1)
         settle(group)
         share(group + 1)
+        if group == 0:
+            send_tokens(0, (2,))
         if group > 0:
             finish(group - 1)
-        if group + 1 == groups:
-            finals = ((gu_m.at[0], fg_ref, gate_rows), (gu_m.at[1], fu_ref, gate_rows),
-                      (d_m, fd_ref, down_rows))
-            for s, j in enumerate(part_peers):
-                for kind, (src, dst, rows) in enumerate(finals):
-                    push(
-                        src.at[:, rows_of(j, rows)], dst.at[heads_of(mine)],
-                        f_s.at[kind, s], f_r.at[kind, s], part_dev(j),
-                    )
-            for src, dst, rows in finals:
-                dst[heads_of(mine)] = src[:, rows_of(mine, rows)]
         wait_share(group + 1)
     apply(groups - 1)
+    for s, j in enumerate(part_peers):
+        for kind, (src, dst) in enumerate(zip(owned(groups, j), finals)):
+            push(src, dst.at[heads_of(mine)], f_s.at[kind, s], f_r.at[kind, s], part_dev(j))
+    for src, dst in zip(owned(groups, mine), finals):
+        dst[heads_of(mine)] = src[...]
     finish(groups - 1)
-    for s in range(parts - 1):
-        j = lax.rem(mine + parts - 1 - s, parts)
-        for kind, (_, dst, rows) in enumerate(finals):
+    for s, j in enumerate(part_peers):
+        for kind, dst in enumerate(finals):
             got = dst.at[heads_of(j)]
             remote(got, got, f_s.at[kind, s], f_r.at[kind, s], part_dev(j)).wait_recv()
+    fg_ref[...] = fin_g[...].astype(jnp.float32)
+    fu_ref[...] = fin_u[...].astype(jnp.float32)
+    fd_ref[...] = fin_d[...].astype(jnp.float32)
     for copy in pending:
         copy.wait_send()
 
@@ -324,6 +346,10 @@
     errors = (value_vectors.astype(jnp.float32) * rate[..., None]).astype(jnp.bfloat16)
 
     bf16, f32 = jnp.bfloat16, jnp.float32
+
+    def wire(rows):
+        return bf16 if rows % 16 == 0 else f32
+
     vmem, dma = pltpu.VMEM, pltpu.SemaphoreType.DMA
     pn, rn, hn = max(parts - 1, 1), max(reps - 1, 1), max(head_n - 1, 1)
     scratch = [
@@ -331,7 +357,12 @@
         vmem((groups, parts, per, block, width), bf16),
         vmem((groups, parts, per, block, width), bf16),
         vmem((groups, pn, per, block, width), bf16),
-        vmem((groups, parts, per, block, width), bf16),
+        vmem(w_gate.shape, wire(gate_rows)),
+        vmem(w_up.shape, wire(gate_rows)),
+        vmem(w_down.shape, wire(down_rows)),
+        vmem(w_gate.shape, wire(gate_rows)),
+        vmem(w_up.shape, wire(gate_rows)),
+        vmem(w_down.shape, wire(down_rows)),
         vmem((2, per, gate_part, width), f32),
         vmem((per, down_part, hidden), f32),
         vmem((groups + 1, 2, per, hidden, width), bf16),
@@ -356,16 +387,17 @@
     ]
     whole = pl.BlockSpec(memory_space=pltpu.VMEM)
     flops = groups * heads * 9 * 2 * block * width * hidden
-    return pl.pallas_call(
+    produced, scale, final_gate, final_up, final_down = pl.pallas_call(
         functools.partial(kernel, (tok_n, head_n, parts, reps, per)),
         out_shape=(
             jax.ShapeDtypeStruct(queries.shape, bf16),
+            jax.ShapeDtypeStruct((groups, block, 128), f32),
             jax.ShapeDtypeStruct(w_gate.shape, f32),
             jax.ShapeDtypeStruct(w_up.shape, f32),
             jax.ShapeDtypeStruct(w_down.shape, f32),
         ),
-        in_specs=[whole] * 8,
-        out_specs=(whole,) * 4,
+        in_specs=[whole] * 7,
+        out_specs=(whole,) * 5,
         scratch_shapes=scratch,
         cost_estimate=pl.CostEstimate(
             flops=flops, bytes_accessed=8 * queries.size, transcendentals=0
@@ -373,7 +405,11 @@
         compiler_params=pltpu.CompilerParams(
             collective_id=0, has_side_effects=True, vmem_limit_bytes=56 * 1024 * 1024
         ),
-    )(key_vectors, errors, queries, mask[..., None], out_gain, w_gate, w_up, w_down)
+    )(key_vectors, errors, queries, mask[..., None], w_gate, w_up, w_down)
+    mixed = (
+        produced.astype(f32) * out_gain[None, :, None, :] * scale[:, None, :, :1]
+    ).astype(bf16)
+    return mixed, final_gate, final_up, final_down
 
 
 def solution(mesh):

time: 188 us -> 180 us (0.957)
  Pallas kernels: 176 us -> 166 us
  other arithmetic: 4.46 us -> 7.95 us
  local copies, waits for them, and re-layouts: 6.14 us -> 4.07 us
    pallas_call x1, Pallas kernels: 176 us -> 166 us  [on_device(): pl.pallas_call(functools.partial(kernel, (tok_n, head_n, parts, reps, per...]
    convert_element_type x0 -> x1, other arithmetic: none -> 3.49 us  [on_device(): mixed = (produced.astype(f32) * out_gain[None, :, None, :] * scale[:, Non...]
    unnamed x12 -> x13, local copies, waits for them, and re-layouts: 5.96 us -> 2.8 us
where the time goes in v2:
time: 180 us; the launch traced here: 179 us
  Pallas kernels  166 us (92%)
  other arithmetic  7.95 us (4%)
  local copies, waits for them, and re-layouts  4.07 us (2%)
    pallas_call x1, Pallas kernels, on_device(): pl.pallas_call(functools.partial(kernel, (tok_n, head_n, parts, reps, per...  166 us

profile of v2, /device:TPU:0, one launch (start us, length us, event | category | flops | bytes accessed | tf_op | source)
XLA Modules:
  0.0 178.6 jit_solution(2583343827216614714)
XLA Ops:
  0.6 0.0 copy-start
  0.6 0.7 copy-done
  1.3 0.2 dynamic-slice_reduce_fusion
  1.5 0.1 compare_select_fusion
  1.6 0.7 convert_multiply_fusion
  2.3 0.8 fusion.mask_ref
  3.1 2.9 %multiply_convert_fusion.1.e_ref = bf16[2,8,256,256]{3,2,1,0:T(8,128)(2,1)} fusion(bf16[2,8,256,256]{3,2,1,0:T(8,128)(2,1)} %param.11, f32[2,8,256]{2,1,0:T(8,128)S(1)} %convert_multiply_fusion), kind=kLoop, calls=%fused_computation.1 | loop fusion | flops 3145728 | bytes 4210688 | tf_op jit(solution)/shard_map/convert_element_type | solution.py:346
  6.0 0.0 copy-start.4
  6.0 165.9 %shard_map.120 = (bf16[2,8,256,256]{3,2,1,0:T(8,128)(2,1)}, f32[2,256,128]{2,1,0:T(8,128)}, f32[8,32,256]{2,1,0:T(8,128)}, f32[8,32,256]{2,1,0:T(8,128)}, f32[8,16,512]{2,1,0:T(8,128)}) custom-call(bf16[2,8,256,256]{3,2,1,0:T(8,128)(2,1)} %k_ref.1, bf16[2,8,256,256]{3,2,1,0:T(8,128)(2,1)} %multiply_convert_fusion.1.e_ref, bf16[2,8,256,256]{3,2,1,0:T(8,128)(2,1)} %q_ref.1, ...), custom_call_target="tpu_custom_call" | custom-call | flops 9663676416 | bytes 8388608 | tf_op jit(solution)/shard_map/pallas_call | solution.py:390
  171.9 1.1 slice_reduce_fusion
  173.0 0.0 copy-done.4
  173.0 0.0 copy-start.3
  173.0 0.0 copy-start.2
  173.0 0.0 copy-start.1
  173.0 3.5 %multiply_convert_fusion = bf16[2,8,256,256]{3,2,1,0:T(8,128)(2,1)} fusion(bf16[2,8,256,256]{3,2,1,0:T(8,128)(2,1)} %get-tuple-element.9, f32[2,256]{1,0:T(2,128)S(1)} %slice_reduce_fusion, f32[8,256]{1,0:T(8,128)S(1)} %copy-done.4), kind=kLoop, calls=%fused_computation | loop fusion | flops 4194304 | bytes 4204544 | tf_op jit(solution)/shard_map/convert_element_type | solution.py:411
  176.5 0.0 copy-done.3
  176.5 0.7 copy.16
  177.2 0.0 copy-done.2
  177.2 0.7 copy.17
  177.9 0.0 copy-done.1
  177.9 0.7 copy.18
Async XLA Ops:
  0.6 0.7 copy-start
  6.0 167.0 %copy-start.4 = (f32[8,256]{1,0:T(8,128)S(1)}, f32[8,256]{1,0:T(8,128)}, u32[]{:S(2)}) copy-start(f32[8,256]{1,0:T(8,128)} %param.14) | copy-start | bytes 24580
  173.0 3.5 %copy-start.3 = (f32[8,32,256]{2,1,0:T(8,128)S(1)}, f32[8,32,256]{2,1,0:T(8,128)}, u32[]{:S(2)}) copy-start(f32[8,32,256]{2,1,0:T(8,128)} %get-tuple-element.19) | copy-start | bytes 786436
  173.0 4.2 %copy-start.2 = (f32[8,32,256]{2,1,0:T(8,128)S(1)}, f32[8,32,256]{2,1,0:T(8,128)}, u32[]{:S(2)}) copy-start(f32[8,32,256]{2,1,0:T(8,128)} %get-tuple-element.20) | copy-start | bytes 786436
  173.0 4.9 %copy-start.1 = (f32[8,16,512]{2,1,0:T(8,128)S(1)}, f32[8,16,512]{2,1,0:T(8,128)}, u32[]{:S(2)}) copy-start(f32[8,16,512]{2,1,0:T(8,128)} %get-tuple-element.21) | copy-start | bytes 786436

commit v3 on v2

--- a/solution.py
+++ b/solution.py
@@ -46,17 +46,18 @@
 
 def kernel(
     dims,
-    k_ref, e_ref, q_ref, mask_ref, wg_ref, wu_ref, wd_ref,
+    cnt_ref, k_ref, v_ref, q_ref, rate_ref, wg_ref, wu_ref, wd_ref,
     out_ref, scale_ref, fg_ref, fu_ref, fd_ref,
-    kbuf, ebuf, qbuf, o_send, wg_c, wu_c, wd_c, fin_g, fin_u, fin_d,
+    e_src, rate_s, kbuf, ebuf, qbuf, o_send, wg_c, wu_c, wd_c, fin_g, fin_u, fin_d,
     gu_m, d_m, gu_b, d_b, dt_b,
     dgu, ddt, dd,
     rs_send, rs_recv, rsd_send, rsd_recv,
     ms_send, ms_recv,
-    tok_s, tok_r, w_s, w_r, o_s, o_r, f_s, f_r,
+    own_s, tok_s, tok_r, w_s, w_r, o_s, o_r, f_s, f_r,
     rs_s, rs_r, ag_s, ag_r, ms_s, ms_r,
 ):
-    tok_n, head_n, parts, reps, per = dims
+    tok_n, head_n, parts, reps, per, grad_scale = dims
+    block = k_ref.shape[2]
     groups = k_ref.shape[0]
     heads = k_ref.shape[1]
     width = k_ref.shape[3]
@@ -89,6 +90,18 @@
     wg_c[...] = wg_ref[...].astype(wg_c.dtype)
     wu_c[...] = wu_ref[...].astype(wu_c.dtype)
     wd_c[...] = wd_ref[...].astype(wd_c.dtype)
+
+    def weigh(group):
+        count = cnt_ref[group, tok]
+        valid = (lax.broadcasted_iota(jnp.int32, (1, block), 1) < count).astype(jnp.float32)
+        rate_s[...] = jnp.zeros_like(rate_s)
+        rate_s[:heads] = rate_ref[group].astype(jnp.float32) * grad_scale * valid
+        columns = rate_s[...].T
+        for head in range(heads):
+            value = v_ref[group, head].astype(jnp.float32)
+            e_src[group, head] = (value * columns[:, head : head + 1]).astype(jnp.bfloat16)
+
+    weigh(0)
     pl.semaphore_wait(barrier, len(everyone))
 
     pending = []
@@ -110,7 +123,7 @@
     def heads_of(index):
         return pl.ds(index * per, per)
 
-    tokens = ((k_ref, kbuf), (e_ref, ebuf), (q_ref, qbuf))
+    tokens = ((k_ref, kbuf), (e_src, ebuf), (q_ref, qbuf))
 
     def send_tokens(group, kinds):
         for s, j in enumerate(part_peers):
@@ -147,20 +160,36 @@
     send_tokens(0, (0, 1))
     for src, dst in zip((wg_c, wu_c, wd_c), owned(0, mine)):
         dst[...] = src[heads_of(mine)]
+    own_copies = []
     for group in range(groups):
-        for src, dst in tokens:
-            dst[group, mine] = src[group, heads_of(mine)]
-
-    def share(stage):
-        gate_own, down_own = rows_of(rep, gate_part), rows_of(rep, down_part)
+        for kind in (0, 2):
+            src, dst = tokens[kind]
+            copy = pltpu.make_async_copy(
+                src.at[group, heads_of(mine)], dst.at[group, mine], own_s.at[group, kind]
+            )
+            copy.start()
+            own_copies.append(copy)
+    ebuf[0, mine] = e_src[0, heads_of(mine)]
+    for group in range(1, groups):
+        weigh(group)
+        ebuf[group, mine] = e_src[group, heads_of(mine)]
+    for copy in own_copies:
+        copy.wait()
+
+    def share_gate(stage):
+        own = rows_of(rep, gate_part)
         if stage > 0 or not narrow_gate:
-            gu_b[stage, :, :, gate_own] = gu_m[...].astype(jnp.bfloat16)
+            gu_b[stage, :, :, own] = gu_m[...].astype(jnp.bfloat16)
+        for s, j in enumerate(rep_peers):
+            gu = gu_b.at[stage, :, :, own]
+            push(gu, gu, ag_s.at[stage, 0, s], ag_r.at[stage, 0, s], rep_dev(j))
+
+    def share_down(stage):
+        own = rows_of(rep, down_part)
         if stage > 0 or not narrow_down:
-            d_b[stage, :, down_own] = d_m[...].astype(jnp.bfloat16)
-        for s, j in enumerate(rep_peers):
-            gu = gu_b.at[stage, :, :, gate_own]
-            push(gu, gu, ag_s.at[stage, 0, s], ag_r.at[stage, 0, s], rep_dev(j))
-            down = d_b.at[stage, :, down_own]
+            d_b[stage, :, own] = d_m[...].astype(jnp.bfloat16)
+        for s, j in enumerate(rep_peers):
+            down = d_b.at[stage, :, own]
             push(down, down, ag_s.at[stage, 1, s], ag_r.at[stage, 1, s], rep_dev(j))
 
     def wait_share(stage):
@@ -177,59 +206,66 @@
         for h in range(per):
             dt_b[h] = d_b[group, h].astype(jnp.float32).T.astype(jnp.bfloat16)
 
-        def one(source):
+        def one(source, rows):
             for h in range(per):
                 key = kbuf[group, source, h]
                 err = ebuf[group, source, h]
-                a = dot_nt(gu_b[group, 0, h], key)
-                b = dot_nt(gu_b[group, 1, h], key)
-                r = dot_nt(dt_b[h], err)
+                a = dot_nt(gu_b[group, 0, h, rows], key)
+                b = dot_nt(gu_b[group, 1, h, rows], key)
+                r = dot_nt(dt_b[h, rows], err)
                 sg = sigmoid(a)
                 act = a * sg
-                ddt[h] += dot_nn((act * b).astype(jnp.bfloat16), err)
+                ddt[h, rows] += dot_nn((act * b).astype(jnp.bfloat16), err)
                 da = (r * b * sg * (1.0 + a * (1.0 - sg))).astype(jnp.bfloat16)
-                dgu[0, h] += dot_nn(da, key)
-                dgu[1, h] += dot_nn((r * act).astype(jnp.bfloat16), key)
-
-        def step(s, carry):
-            source = flip(mine, s, parts)
-
-            @pl.when(s > 0)
-            def _():
-                wait_tokens(group, (0, 1), source, s - 1)
-
-            one(source)
-            return carry
-
-        lax.fori_loop(0, parts, step, 0)
-        for h in range(per):
-            dd[h] = ddt[h].T
-
-    def scatter(group):
-        for s, j in enumerate(rep_peers):
-            rs_send[group, s] = dgu[:, :, rows_of(j, gate_part)].astype(jnp.bfloat16)
+                dgu[0, h, rows] += dot_nn(da, key)
+                dgu[1, h, rows] += dot_nn((r * act).astype(jnp.bfloat16), key)
+
+        def one_pass(rows, first):
+            def step(s, carry):
+                source = flip(mine, s, parts)
+                if first:
+
+                    @pl.when(s > 0)
+                    def _():
+                        wait_tokens(group, (0, 1), source, s - 1)
+
+                one(source, rows)
+                return carry
+
+            lax.fori_loop(0, parts, step, 0)
+
+        for s, j in enumerate(rep_peers):
+            rows = rows_of(j, gate_part)
+            one_pass(rows, s == 0)
+            rs_send[group, s] = dgu[:, :, rows].astype(jnp.bfloat16)
             push(
                 rs_send.at[group, s], rs_recv.at[group, s],
                 rs_s.at[group, 0, s], rs_r.at[group, 0, s], rep_dev(j),
             )
+        one_pass(rows_of(rep, gate_part), not rep_peers)
+        for h in range(per):
+            dd[h] = ddt[h].T
+        for s, j in enumerate(rep_peers):
             rsd_send[group, s] = dd[:, rows_of(j, down_part)].astype(jnp.bfloat16)
             push(
                 rsd_send.at[group, s], rsd_recv.at[group, s],
                 rs_s.at[group, 1, s], rs_r.at[group, 1, s], rep_dev(j),
             )
 
-    def settle(group):
+    def settle_gate(group):
         gate = gu_m[...] + dgu[:, :, rows_of(rep, gate_part)]
-        down = d_m[...] + dd[:, rows_of(rep, down_part)]
-        for s in range(reps - 1):
-            j = rep_peers[s]
+        for s, j in enumerate(rep_peers):
             got = rs_recv.at[group, s]
             remote(got, got, rs_s.at[group, 0, s], rs_r.at[group, 0, s], rep_dev(j)).wait_recv()
             gate = gate + got[...].astype(jnp.float32)
+        gu_m[...] = renorm(gu_m[...], gate)
+
+    def settle_down(group):
+        down = d_m[...] + dd[:, rows_of(rep, down_part)]
+        for s, j in enumerate(rep_peers):
             got = rsd_recv.at[group, s]
             remote(got, got, rs_s.at[group, 1, s], rs_r.at[group, 1, s], rep_dev(j)).wait_recv()
             down = down + got[...].astype(jnp.float32)
-        gu_m[...] = renorm(gu_m[...], gate)
         d_m[...] = renorm(d_m[...], down)
 
     def apply(group):
@@ -283,13 +319,16 @@
             remote(got, got, ms_s.at[group, s], ms_r.at[group, s], (j, tok)).wait_recv()
             total = total + got[...]
         mean = jnp.sum(total, axis=1, keepdims=True) / (head_n * heads * width)
-        scale = lax.rsqrt(mean + epsilon) * mask_ref[group]
-        scale_ref[group] = jnp.broadcast_to(scale, scale_ref.shape[1:])
+        scale = lax.rsqrt(mean + epsilon) * (
+            lax.broadcasted_iota(jnp.int32, (block, 1), 0) < cnt_ref[group, tok]
+        ).astype(jnp.float32)
+        scale_ref[group] = scale
 
     for s, j in enumerate(part_peers):
         for kind, got in enumerate(owned(0, j)):
             remote(got, got, w_s.at[kind, s], w_r.at[kind, s], part_dev(j)).wait_recv()
-    share(0)
+    share_gate(0)
+    share_down(0)
     if narrow_gate:
         gu_m[...] = gu_b[0, :, :, rows_of(rep, gate_part)].astype(jnp.float32)
     if narrow_down:
@@ -298,25 +337,27 @@
     finals = (fin_g, fin_u, fin_d)
     for group in range(groups):
         update(group)
-        scatter(group)
         if group + 1 < groups:
             send_tokens(group + 1, (0, 1))
         if group > 0:
             send_tokens(group, (2,))
             apply(group - 1)
-        settle(group)
-        share(group + 1)
+        settle_gate(group)
+        share_gate(group + 1)
+        settle_down(group)
+        share_down(group + 1)
         if group == 0:
             send_tokens(0, (2,))
+        if group + 1 == groups:
+            for s, j in enumerate(part_peers):
+                for kind, (src, dst) in enumerate(zip(owned(groups, j), finals)):
+                    push(src, dst.at[heads_of(mine)], f_s.at[kind, s], f_r.at[kind, s], part_dev(j))
+            for src, dst in zip(owned(groups, mine), finals):
+                dst[heads_of(mine)] = src[...]
         if group > 0:
             finish(group - 1)
         wait_share(group + 1)
     apply(groups - 1)
-    for s, j in enumerate(part_peers):
-        for kind, (src, dst) in enumerate(zip(owned(groups, j), finals)):
-            push(src, dst.at[heads_of(mine)], f_s.at[kind, s], f_r.at[kind, s], part_dev(j))
-    for src, dst in zip(owned(groups, mine), finals):
-        dst[heads_of(mine)] = src[...]
     finish(groups - 1)
     for s, j in enumerate(part_peers):
         for kind, dst in enumerate(finals):
@@ -340,11 +381,6 @@
     gate_rows, down_rows = w_gate.shape[1], w_down.shape[1]
     gate_part, down_part = parts * gate_rows, parts * down_rows
     grad_scale = float(tok_n * block) ** (-0.5)
-    own = lax.dynamic_slice_in_dim(counts, lax.axis_index("tok"), 1, 1)
-    mask = (jnp.arange(block, dtype=jnp.int32)[None, :] < own).astype(jnp.float32)
-    rate = step_rates.astype(jnp.float32) * grad_scale * mask[:, None, :]
-    errors = (value_vectors.astype(jnp.float32) * rate[..., None]).astype(jnp.bfloat16)
-
     bf16, f32 = jnp.bfloat16, jnp.float32
 
     def wire(rows):
@@ -353,6 +389,8 @@
     vmem, dma = pltpu.VMEM, pltpu.SemaphoreType.DMA
     pn, rn, hn = max(parts - 1, 1), max(reps - 1, 1), max(head_n - 1, 1)
     scratch = [
+        vmem(value_vectors.shape, bf16),
+        vmem((max(8, heads), block), f32),
         vmem((groups, parts, per, block, width), bf16),
         vmem((groups, parts, per, block, width), bf16),
         vmem((groups, parts, per, block, width), bf16),
@@ -377,6 +415,7 @@
         vmem((groups, rn, per, down_part, hidden), bf16),
         vmem((groups, block, width // 2), f32),
         vmem((groups, hn, block, width // 2), f32),
+        dma((groups, 3)),
         dma((groups, 3, pn)), dma((groups, 3, pn)),
         dma((3, pn)), dma((3, pn)),
         dma((groups, pn)), dma((groups, pn)),
@@ -386,17 +425,18 @@
         dma((groups, hn)), dma((groups, hn)),
     ]
     whole = pl.BlockSpec(memory_space=pltpu.VMEM)
+    hbm = pl.BlockSpec(memory_space=pl.ANY)
     flops = groups * heads * 9 * 2 * block * width * hidden
     produced, scale, final_gate, final_up, final_down = pl.pallas_call(
-        functools.partial(kernel, (tok_n, head_n, parts, reps, per)),
+        functools.partial(kernel, (tok_n, head_n, parts, reps, per, grad_scale)),
         out_shape=(
             jax.ShapeDtypeStruct(queries.shape, bf16),
-            jax.ShapeDtypeStruct((groups, block, 128), f32),
+            jax.ShapeDtypeStruct((groups, block, 1), f32),
             jax.ShapeDtypeStruct(w_gate.shape, f32),
             jax.ShapeDtypeStruct(w_up.shape, f32),
             jax.ShapeDtypeStruct(w_down.shape, f32),
         ),
-        in_specs=[whole] * 7,
+        in_specs=[pl.BlockSpec(memory_space=pltpu.SMEM), hbm, whole, hbm] + [whole] * 4,
         out_specs=(whole,) * 5,
         scratch_shapes=scratch,
         cost_estimate=pl.CostEstimate(
@@ -405,9 +445,9 @@
         compiler_params=pltpu.CompilerParams(
             collective_id=0, has_side_effects=True, vmem_limit_bytes=56 * 1024 * 1024
         ),
-    )(key_vectors, errors, queries, mask[..., None], w_gate, w_up, w_down)
+    )(counts, key_vectors, value_vectors, queries, step_rates, w_gate, w_up, w_down)
     mixed = (
-        produced.astype(f32) * out_gain[None, :, None, :] * scale[:, None, :, :1]
+        produced.astype(f32) * out_gain[None, :, None, :] * scale[:, None]
     ).astype(bf16)
     return mixed, final_gate, final_up, final_down
 

time: 180 us -> 176 us (0.978)
  other arithmetic: 7.95 us -> 4.58 us
  Pallas kernels: 166 us -> 169 us
  local copies, waits for them, and re-layouts: 4.07 us -> 2.12 us
    convert_element_type x2 -> x0, other arithmetic: 3.68 us -> none  [the longest x1 2.89 us: on_device(): (value_vectors.astype(jnp.float32) * rate[..., None]).astype(jnp.bfloat16)]
    pallas_call x1, Pallas kernels: 166 us -> 169 us  [on_device(): pl.pallas_call(functools.partial(kernel, (tok_n, head_n, parts, reps, per...]
where the time goes in v3:
time: 176 us
  Pallas kernels  169 us (96%)
  other arithmetic  4.58 us (3%)
  local copies, waits for them, and re-layouts  2.12 us (1%)
    pallas_call x1, Pallas kernels, on_device(): pl.pallas_call(functools.partial(kernel, (tok_n, head_n, parts, reps, per...  169 us

profile of v3, /device:TPU:0, one launch (start us, length us, event | category | flops | bytes accessed | tf_op | source)
XLA Modules:
  0.0 176.0 jit_solution(18238394976283631726)
XLA Ops:
  0.6 0.0 copy-start.3
  0.6 168.6 %shard_map.120 = (bf16[2,8,256,256]{3,2,1,0:T(8,128)(2,1)}, f32[2,256,1]{2,1,0:T(8,128)}, f32[8,32,256]{2,1,0:T(8,128)}, f32[8,32,256]{2,1,0:T(8,128)}, f32[8,16,512]{2,1,0:T(8,128)}) custom-call(s32[2,16]{1,0:T(2,128)} %cnt_ref.1, bf16[2,8,256,256]{3,2,1,0:T(8,128)(2,1)} %k_ref.1, bf16[2,8,256,256]{3,2,1,0:T(8,128)(2,1)} %v_ref.1, ...), custom_call_target="tpu_custom_call" | custom-call | flops 9663676416 | bytes 8388608 | tf_op jit(solution)/shard_map/pallas_call | solution.py:430
  169.3 1.1 reduce
  170.4 0.0 copy-done.3
  170.4 0.0 copy-start.2
  170.4 0.0 copy-start.1
  170.4 0.0 copy-start
  170.4 3.5 %multiply_convert_fusion = bf16[2,8,256,256]{3,2,1,0:T(8,128)(2,1)} fusion(bf16[2,8,256,256]{3,2,1,0:T(8,128)(2,1)} %get-tuple-element.9, f32[2,256]{1,0:T(2,128)S(1)} %reduce, f32[8,256]{1,0:T(8,128)S(1)} %copy-done.3), kind=kLoop, calls=%fused_computation | loop fusion | flops 4194304 | bytes 4204544 | tf_op jit(solution)/shard_map/convert_element_type | solution.py:451
  173.9 0.0 copy-done.2
  173.9 0.7 copy.16
  174.6 0.0 copy-done.1
  174.6 0.7 copy.17
  175.3 0.0 copy-done
  175.3 0.7 copy.18
Async XLA Ops:
  0.6 169.7 %copy-start.3 = (f32[8,256]{1,0:T(8,128)S(1)}, f32[8,256]{1,0:T(8,128)}, u32[]{:S(2)}) copy-start(f32[8,256]{1,0:T(8,128)} %param.14) | copy-start | bytes 24580
  170.4 3.5 %copy-start.2 = (f32[8,32,256]{2,1,0:T(8,128)S(1)}, f32[8,32,256]{2,1,0:T(8,128)}, u32[]{:S(2)}) copy-start(f32[8,32,256]{2,1,0:T(8,128)} %get-tuple-element.19) | copy-start | bytes 786436
  170.4 4.2 %copy-start.1 = (f32[8,32,256]{2,1,0:T(8,128)S(1)}, f32[8,32,256]{2,1,0:T(8,128)}, u32[]{:S(2)}) copy-start(f32[8,32,256]{2,1,0:T(8,128)} %get-tuple-element.20) | copy-start | bytes 786436
  170.4 4.9 %copy-start = (f32[8,16,512]{2,1,0:T(8,128)S(1)}, f32[8,16,512]{2,1,0:T(8,128)}, u32[]{:S(2)}) copy-start(f32[8,16,512]{2,1,0:T(8,128)} %get-tuple-element.21) | copy-start | bytes 786436

commit v4 on v3

--- a/solution.py
+++ b/solution.py
@@ -200,7 +200,7 @@
             down = d_b.at[stage, :, rows_of(j, down_part)]
             remote(down, down, ag_s.at[stage, 1, s], ag_r.at[stage, 1, s], rep_dev(j)).wait_recv()
 
-    def update(group):
+    def update(group, between):
         dgu[...] = jnp.zeros_like(dgu)
         ddt[...] = jnp.zeros_like(ddt)
         for h in range(per):
@@ -242,6 +242,7 @@
                 rs_send.at[group, s], rs_recv.at[group, s],
                 rs_s.at[group, 0, s], rs_r.at[group, 0, s], rep_dev(j),
             )
+        between()
         one_pass(rows_of(rep, gate_part), not rep_peers)
         for h in range(per):
             dd[h] = ddt[h].T
@@ -299,30 +300,33 @@
             pending.append(out_copy(s))
 
     def finish(group):
-        for s, j in enumerate(part_peers):
+        half = width // 2
+
+        def squares(total, source):
+            for h in range(per):
+                o = out_ref[group, source * per + h].astype(jnp.float32)
+                total = total + (o[:, :half] * o[:, :half] + o[:, half:] * o[:, half:])
+            return total
+
+        total = squares(jnp.zeros((block, half), jnp.float32), mine)
+        for s, j in reversed(list(enumerate(part_peers))):
             got = out_ref.at[group, heads_of(j)]
             remote(got, got, o_s.at[group, s], o_r.at[group, s], part_dev(j)).wait_recv()
-        half = width // 2
-        total = jnp.zeros((k_ref.shape[2], half), jnp.float32)
-        for head in range(heads):
-            o = out_ref[group, head].astype(jnp.float32)
-            total = total + (o[:, :half] * o[:, :half] + o[:, half:] * o[:, half:])
-        ms_send[group] = total
+            total = squares(total, j)
+        row = jnp.sum(total.T, axis=0, keepdims=True)
+        ms_send[group] = jnp.broadcast_to(row, ms_send.shape[1:])
         for s, j in enumerate(head_peers):
             push(
                 ms_send.at[group], ms_recv.at[group, s],
                 ms_s.at[group, s], ms_r.at[group, s], (j, tok),
             )
-        for s in range(head_n - 1):
-            j = head_peers[s]
+        for s, j in enumerate(head_peers):
             got = ms_recv.at[group, s]
             remote(got, got, ms_s.at[group, s], ms_r.at[group, s], (j, tok)).wait_recv()
-            total = total + got[...]
-        mean = jnp.sum(total, axis=1, keepdims=True) / (head_n * heads * width)
-        scale = lax.rsqrt(mean + epsilon) * (
-            lax.broadcasted_iota(jnp.int32, (block, 1), 0) < cnt_ref[group, tok]
-        ).astype(jnp.float32)
-        scale_ref[group] = scale
+            row = row + got[:1]
+        valid = lax.broadcasted_iota(jnp.int32, (1, block), 1) < cnt_ref[group, tok]
+        mean = row / (head_n * heads * width)
+        scale_ref[pl.ds(group, 1), :] = lax.rsqrt(mean + epsilon) * valid.astype(jnp.float32)
 
     for s, j in enumerate(part_peers):
         for kind, got in enumerate(owned(0, j)):
@@ -336,11 +340,14 @@
     wait_share(0)
     finals = (fin_g, fin_u, fin_d)
     for group in range(groups):
-        update(group)
-        if group + 1 < groups:
-            send_tokens(group + 1, (0, 1))
+        def between():
+            if group + 1 < groups:
+                send_tokens(group + 1, (0, 1))
+            if group > 0:
+                send_tokens(group, (2,))
+
+        update(group, between)
         if group > 0:
-            send_tokens(group, (2,))
             apply(group - 1)
         settle_gate(group)
         share_gate(group + 1)
@@ -413,8 +420,8 @@
         vmem((groups, rn, 2, per, gate_part, width), bf16),
         vmem((groups, rn, per, down_part, hidden), bf16),
         vmem((groups, rn, per, down_part, hidden), bf16),
-        vmem((groups, block, width // 2), f32),
-        vmem((groups, hn, block, width // 2), f32),
+        vmem((groups, 8, block), f32),
+        vmem((groups, hn, 8, block), f32),
         dma((groups, 3)),
         dma((groups, 3, pn)), dma((groups, 3, pn)),
         dma((3, pn)), dma((3, pn)),
@@ -431,7 +438,7 @@
         functools.partial(kernel, (tok_n, head_n, parts, reps, per, grad_scale)),
         out_shape=(
             jax.ShapeDtypeStruct(queries.shape, bf16),
-            jax.ShapeDtypeStruct((groups, block, 1), f32),
+            jax.ShapeDtypeStruct((groups, block), f32),
             jax.ShapeDtypeStruct(w_gate.shape, f32),
             jax.ShapeDtypeStruct(w_up.shape, f32),
             jax.ShapeDtypeStruct(w_down.shape, f32),
@@ -447,7 +454,7 @@
         ),
     )(counts, key_vectors, value_vectors, queries, step_rates, w_gate, w_up, w_down)
     mixed = (
-        produced.astype(f32) * out_gain[None, :, None, :] * scale[:, None]
+        produced.astype(f32) * out_gain[None, :, None, :] * scale[:, None, :, None]
     ).astype(bf16)
     return mixed, final_gate, final_up, final_down
 

time: 176 us -> 169 us (0.960)
  Pallas kernels: 169 us -> 163 us
    pallas_call x1, Pallas kernels: 169 us -> 163 us  [on_device(): pl.pallas_call(functools.partial(kernel, (tok_n, head_n, parts, reps, per...]
where the time goes in v4:
time: 169 us
  Pallas kernels  163 us (96%)
  other arithmetic  3.54 us (2%)
  local copies, waits for them, and re-layouts  2.12 us (1%)
    pallas_call x1, Pallas kernels, on_device(): pl.pallas_call(functools.partial(kernel, (tok_n, head_n, parts, reps, per...  163 us
    convert_element_type x1, other arithmetic, on_device(): mixed = (produced.astype(f32) * out_gain[None, :, None, :] * scale[:, Non...  3.54 us

profile of v4, /device:TPU:0, one launch (start us, length us, event | category | flops | bytes accessed | tf_op | source)
XLA Modules:
  0.0 169.1 jit_solution(3925251883600777950)
XLA Ops:
  0.6 0.0 copy-start.3
  0.6 162.8 %shard_map.120 = (bf16[2,8,256,256]{3,2,1,0:T(8,128)(2,1)}, f32[2,256]{1,0:T(2,128)}, f32[8,32,256]{2,1,0:T(8,128)}, f32[8,32,256]{2,1,0:T(8,128)}, f32[8,16,512]{2,1,0:T(8,128)}) custom-call(s32[2,16]{1,0:T(2,128)} %cnt_ref.1, bf16[2,8,256,256]{3,2,1,0:T(8,128)(2,1)} %k_ref.1, bf16[2,8,256,256]{3,2,1,0:T(8,128)(2,1)} %v_ref.1, ...), custom_call_target="tpu_custom_call" | custom-call | flops 9663676416 | bytes 8388608 | tf_op jit(solution)/shard_map/pallas_call | solution.py:437
  163.4 0.0 copy-done.3
  163.4 0.0 copy-start.2
  163.4 0.0 copy-start.1
  163.5 0.0 copy-start
  163.5 3.5 %multiply_convert_fusion = bf16[2,8,256,256]{3,2,1,0:T(8,128)(2,1)} fusion(bf16[2,8,256,256]{3,2,1,0:T(8,128)(2,1)} %get-tuple-element.9, f32[2,256]{1,0:T(2,128)} %get-tuple-element.10, f32[8,256]{1,0:T(8,128)S(1)} %copy-done.3), kind=kLoop, calls=%fused_computation | loop fusion | flops 4194304 | bytes 4204544 | tf_op jit(solution)/shard_map/convert_element_type | solution.py:458
  167.0 0.0 copy-done.2
  167.0 0.7 copy.16
  167.7 0.0 copy-done.1
  167.7 0.7 copy.17
  168.4 0.0 copy-done
  168.4 0.7 copy.18
Async XLA Ops:
  0.6 162.8 %copy-start.3 = (f32[8,256]{1,0:T(8,128)S(1)}, f32[8,256]{1,0:T(8,128)}, u32[]{:S(2)}) copy-start(f32[8,256]{1,0:T(8,128)} %param.14) | copy-start | bytes 24580
  163.4 3.6 %copy-start.2 = (f32[8,32,256]{2,1,0:T(8,128)S(1)}, f32[8,32,256]{2,1,0:T(8,128)}, u32[]{:S(2)}) copy-start(f32[8,32,256]{2,1,0:T(8,128)} %get-tuple-element.19) | copy-start | bytes 786436
  163.4 4.3 %copy-start.1 = (f32[8,32,256]{2,1,0:T(8,128)S(1)}, f32[8,32,256]{2,1,0:T(8,128)}, u32[]{:S(2)}) copy-start(f32[8,32,256]{2,1,0:T(8,128)} %get-tuple-element.20) | copy-start | bytes 786436
  163.5 5.0 %copy-start = (f32[8,16,512]{2,1,0:T(8,128)S(1)}, f32[8,16,512]{2,1,0:T(8,128)}, u32[]{:S(2)}) copy-start(f32[8,16,512]{2,1,0:T(8,128)} %get-tuple-element.21) | copy-start | bytes 786436
